TPU v7x, 32 devices: a whole 2x2x4 slice. The times are simulated.
32 devices in a mesh: grid: 8 (over z, x), cols: 4 (over y, core).
Axes of the slice: x: 2, y: 2, z: 4, core: 2. Of those that a mesh axis runs over, the one named last changes fastest.
Arguments:
- basis: float32 [1024, 3, 16, 1024], P('cols', None, 'grid'), may hold values from -1 to 1
- snapshots: float32 [128, 3, 16, 1024], P('cols', None, 'grid'), may hold values from -60 to 60
- permittivity: float32 [3, 16, 1024], P(None, 'grid'), may hold values from 1 to 10
- labels: int32 [16, 1024], P('grid'), may hold values from 0 to 7
- sigma_table: float32 [8], replicated, may hold values from 0.1 to 10
Outputs:
- new_basis: float32 [128, 3, 16, 1024], P('cols', None, 'grid')
- coefficients: float32 [1024, 128], P('cols')
- cross_terms: float32 [3, 1024, 128], P(None, 'cols')
- block_terms: float32 [3, 128, 128], P(None, 'cols')
All inputs are finite; a program needn't handle non-finite values.
Results may differ from a plain program's by a relative error of at most 0.0003.
Values sent between devices are 32-bit elements; how exact they have to be, the bound alone decides.
A program may use at most 128 MiB of HBM per device.

v0:
```python
import jax
import jax.numpy as jnp
from jax import lax
from jax.sharding import PartitionSpec as P

NY = 32
HIGHEST = lax.Precision.HIGHEST


def padded(shard, sides, width):
    for axis, dim in sides:
        size, length = (lax.axis_size(axis), shard.shape[dim])
        up = [(i, (i + 1) % size) for i in range(size - 1)]
        down = [(j, i) for i, j in up]
        last = lax.slice_in_dim(shard, length - width, length, axis=dim)
        leading = lax.slice_in_dim(shard, 0, width, axis=dim)
        before = lax.ppermute(last, axis, up)
        after = lax.ppermute(leading, axis, down)
        shard = jnp.concatenate([before, shard, after], axis=dim)
    return shard


def cells_dot(left_rows, right_rows):
    left_flat = left_rows.reshape(left_rows.shape[0], -1)
    right_flat = right_rows.reshape(right_rows.shape[0], -1)
    return lax.dot_general(
        left_flat,
        right_flat,
        (((1,), (1,)), ((), ())),
        precision=HIGHEST,
        preferred_element_type=jnp.float32,
    )


def combine_rows(weights, fields):
    flattened = fields.reshape(fields.shape[0], -1)
    output_rows = lax.dot_general(
        weights,
        flattened,
        (((0,), (0,)), ((), ())),
        precision=HIGHEST,
        preferred_element_type=jnp.float32,
    )
    return output_rows.reshape((weights.shape[1],) + fields.shape[1:])


def forward_x(field, row_len):
    padding_cols = jnp.zeros(field.shape[:-1] + (row_len,), field.dtype)
    return jnp.concatenate([field[..., row_len:], padding_cols], axis=-1)


def backward_x(field, row_len):
    padding_cols = jnp.zeros(field.shape[:-1] + (row_len,), field.dtype)
    return jnp.concatenate([padding_cols, field[..., :-row_len]], axis=-1)


def forward_y(field, row_len):
    column_pos = lax.broadcasted_iota(jnp.int32, (field.shape[-1],), 0) % row_len
    padding_cols = jnp.zeros(field.shape[:-1] + (1,), field.dtype)
    shifted = jnp.concatenate([field[..., 1:], padding_cols], axis=-1)
    return jnp.where(column_pos != row_len - 1, shifted, 0.0)


def backward_y(field, row_len):
    column_pos = lax.broadcasted_iota(jnp.int32, (field.shape[-1],), 0) % row_len
    padding_cols = jnp.zeros(field.shape[:-1] + (1,), field.dtype)
    shifted = jnp.concatenate([padding_cols, field[..., :-1]], axis=-1)
    return jnp.where(column_pos != 0, shifted, 0.0)


def curl_curl(extended, row_len):
    field_x = extended[:, 0]
    field_y = extended[:, 1]
    field_z = extended[:, 2]

    def middle(field):
        return field[:, 1:-1]

    def plus_x(field):
        return forward_x(field, row_len) - field

    def minus_x(field):
        return field - backward_x(field, row_len)

    def plus_y(field):
        return forward_y(field, row_len) - field

    def minus_y(field):
        return field - backward_y(field, row_len)

    def second_x(field):
        return forward_x(field, row_len) - 2.0 * field + backward_x(field, row_len)

    def second_y(field):
        return forward_y(field, row_len) - 2.0 * field + backward_y(field, row_len)

    def second_z(field):
        return field[:, 2:] - 2.0 * field[:, 1:-1] + field[:, :-2]

    curl_x = (
        -second_y(middle(field_x))
        - second_z(field_x)
        + minus_y(plus_x(middle(field_y)))
        + plus_x(middle(field_z))
        - plus_x(field_z[:, :-2])
    )
    curl_y = (
        -second_x(middle(field_y))
        - second_z(field_y)
        + minus_x(plus_y(middle(field_x)))
        + plus_y(middle(field_z))
        - plus_y(field_z[:, :-2])
    )
    curl_z = (
        -second_x(middle(field_z))
        - second_y(middle(field_z))
        + minus_x(field_x[:, 2:] - middle(field_x))
        + minus_y(field_y[:, 2:] - middle(field_y))
    )
    return jnp.stack([curl_x, curl_y, curl_z], axis=1)


def lookup_sigma(labels, sigma_table):
    region_ids = jnp.arange(sigma_table.shape[0], dtype=jnp.int32)
    picked = jnp.where(labels[None] == region_ids[:, None, None], sigma_table[:, None, None], 0.0)
    return jnp.sum(picked, axis=0)


def apply_ops(fields, permittivity, conductivity):
    extended = padded(fields, (("grid", 2),), 1)
    curl_term = curl_curl(extended, NY)
    mass_term = permittivity[None] * fields
    loss_term = conductivity[None, None] * fields
    return (curl_term, mass_term, loss_term)


def shards(basis, snapshots, permittivity, labels, sigma_table):
    basis_cols = basis.shape[0]
    snap_cols = snapshots.shape[0]
    total_snap = snap_cols * lax.axis_size("cols")
    unknowns = 3 * snapshots.shape[3] * snapshots.shape[2] * lax.axis_size("grid")
    conductivity = lookup_sigma(labels, sigma_table)
    current = snapshots
    coefficients = jnp.zeros((basis_cols, total_snap), jnp.float32)
    for sweep_index in range(2):
        partial_value = cells_dot(basis, lax.all_gather(current, "cols", axis=0, tiled=True))
        coef_part = lax.psum(partial_value, "grid")
        current = current - lax.psum_scatter(
            combine_rows(coef_part, basis), "cols", scatter_dimension=0, tiled=True
        )
        coefficients = coefficients + coef_part
    finished = lax.all_gather(current, "cols", axis=0, tiled=True)
    own_start = lax.axis_index("cols") * snap_cols
    identity = jnp.eye(total_snap, dtype=jnp.float32)
    gram_sum = lax.psum(cells_dot(finished, finished) / unknowns, "grid")
    lower_factor = jnp.linalg.cholesky(gram_sum)
    inverse = jax.scipy.linalg.solve_triangular(lower_factor, identity, lower=True)
    new_all = combine_rows(inverse.T, finished)
    curl_term, mass_term, loss_term = apply_ops(new_all, permittivity, conductivity)
    own_new = lax.dynamic_slice_in_dim(new_all, own_start, snap_cols, 0)
    cross_part = jnp.stack(
        [cells_dot(basis, curl_term), cells_dot(basis, mass_term), cells_dot(basis, loss_term)],
        axis=0,
    )
    block_part = (
        jnp.stack(
            [
                cells_dot(own_new, curl_term),
                cells_dot(own_new, mass_term),
                cells_dot(own_new, loss_term),
            ],
            axis=0,
        )
        / unknowns
    )
    cross_terms, block_terms = lax.psum((cross_part, block_part), "grid")
    return (own_new, coefficients, cross_terms, block_terms)


def solution(mesh):
    placed = (
        P("cols", None, "grid", None),
        P("cols", None, "grid", None),
        P(None, "grid", None),
        P("grid", None),
        P(),
    )
    return jax.shard_map(
        shards,
        mesh=mesh,
        in_specs=placed,
        out_specs=(
            P("cols", None, "grid", None),
            P("cols", None),
            P(None, "cols", None),
            P(None, "cols", None),
        ),
        check_vma=False,
    )
```

profile of v0, /device:TPU:0, one launch (start us, length us, event | category | flops | bytes accessed | tf_op | source)
XLA Modules:
  0.0 642.6 jit_solution(8649278137576237144)
XLA Ops:
  9.5 31.9 %all-gather.4.cloned.1.call-done = f32[128,3,2,1024]{3,0,2,1:T(8,128)} async-done(((f32[32,3,2,1024]{3,0,2,1:T(8,128)}), f32[128,3,2,1024]{3,0,2,1:T(8,128)}) %all-gather.4.cloned.1.call-update) | async-done | bytes 3145744 | tf_op jit(solution)/shard_map/all_gather | solution.py:146
  41.4 10.8 %fusion.23 = f32[256,128]{1,0:T(8,128)} fusion(f32[128,3,2,1024]{3,0,2,1:T(8,128)} %all-gather.4.cloned.1.call-done, f32[256,3,2,1024]{3,2,1,0:T(2,128)} %param.5), kind=kOutput, calls=%fused_computation.28 | convolution fusion | flops 2415919104 | bytes 9568256 | tf_op jit(solution)/shard_map/dot_general | solution.py:26
  52.2 9.0 %reshape.49 = f32[256,6144]{1,0:T(8,128)} reshape(f32[256,3,2,1024]{3,2,1,0:T(2,128)} %param.5) | data formatting | bytes 12582912 | tf_op jit(solution)/shard_map/reshape | solution.py:24
  61.2 6.6 %copy.42 = f32[6144,256]{1,0:T(8,128)} copy(f32[6144,256]{0,1:T(8,128)} %bitcast.112) | data formatting | bytes 12582912 | tf_op jit(solution)/shard_map/dot_general | solution.py:37
  67.8 54.2 %all-reduce.19.cloned.1.call-done = f32[256,128]{1,0:T(8,128)} async-done(((f32[256,128]{1,0:T(8,128)}), f32[256,128]{1,0:T(8,128)}) %all-reduce.19.cloned.1.call-update) | async-done | bytes 131088 | tf_op jit(solution)/shard_map/psum | solution.py:147
  122.0 11.2 %fusion.63 = f32[128,3,2,1024]{3,0,2,1:T(8,128)} fusion(f32[3,2,1024,256]{3,2,1,0:T(8,128)} %bitcast.110, f32[256,128]{1,0:T(8,128)} %all-reduce.19.cloned.1.call-done), kind=kOutput, calls=%fused_computation.61 | convolution fusion | flops 2415919104 | bytes 9568256 | tf_op jit(solution)/shard_map/dot_general | solution.py:37
  133.6 37.1 %reduce-scatter.3.cloned.1.call-done = f32[32,3,2,1024]{3,0,2,1:T(8,128)} async-done(((f32[128,3,2,1024]{3,0,2,1:T(8,128)}), f32[32,3,2,1024]{3,0,2,1:T(8,128)}) %reduce-scatter.3.cloned.1.call-update) | async-done | bytes 786448 | tf_op jit(solution)/shard_map/reduce_scatter | solution.py:148
  173.1 28.6 %all-gather.6.cloned.1.call-done = f32[128,3,2,1024]{3,0,2,1:T(8,128)} async-done(((f32[32,3,2,1024]{3,0,2,1:T(8,128)}), f32[128,3,2,1024]{3,0,2,1:T(8,128)}) %all-gather.6.cloned.1.call-update) | async-done | bytes 3145744 | tf_op jit(solution)/shard_map/all_gather | solution.py:146
  201.7 10.7 %fusion.26 = f32[256,128]{1,0:T(8,128)} fusion(f32[128,3,2,1024]{3,0,2,1:T(8,128)} %all-gather.6.cloned.1.call-done, f32[256,3,2,1024]{3,2,1,0:T(2,128)} %param.5), kind=kOutput, calls=%fused_computation.29 | convolution fusion | flops 2415919104 | bytes 9568256 | tf_op jit(solution)/shard_map/dot_general | solution.py:26
  212.4 69.8 %all-reduce.21.cloned.1.call-done = f32[256,128]{1,0:T(8,128)} async-done(((f32[256,128]{1,0:T(8,128)}), f32[256,128]{1,0:T(8,128)}) %all-reduce.21.cloned.1.call-update) | async-done | bytes 131088 | tf_op jit(solution)/shard_map/psum | solution.py:147
  282.2 11.2 %fusion.61 = f32[128,3,2,1024]{3,0,2,1:T(8,128)} fusion(f32[3,2,1024,256]{3,2,1,0:T(8,128)} %bitcast.111, f32[256,128]{1,0:T(8,128)} %all-reduce.21.cloned.1.call-done), kind=kOutput, calls=%fused_computation.59 | convolution fusion | flops 2415919104 | bytes 9568256 | tf_op jit(solution)/shard_map/dot_general | solution.py:37
  293.5 37.3 %reduce-scatter.5.cloned.1.call-done = f32[32,3,2,1024]{3,0,2,1:T(8,128)} async-done(((f32[128,3,2,1024]{3,0,2,1:T(8,128)}), f32[32,3,2,1024]{3,0,2,1:T(8,128)}) %reduce-scatter.5.cloned.1.call-update) | async-done | bytes 786448 | tf_op jit(solution)/shard_map/reduce_scatter | solution.py:148
  333.4 28.2 %all-gather.8.cloned.1.call-done = f32[128,3,2,1024]{3,0,2,1:T(8,128)} async-done(((f32[32,3,2,1024]{3,0,2,1:T(8,128)}), f32[128,3,2,1024]{3,0,2,1:T(8,128)}) %all-gather.8.cloned.1.call-update) | async-done | bytes 3145744 | tf_op jit(solution)/shard_map/all_gather | solution.py:152
  361.7 6.3 fusion.42
  370.4 66.2 %all-reduce.23.cloned.1.call-done = f32[128,128]{0,1:T(8,128)} async-done(((f32[128,128]{0,1:T(8,128)}), f32[128,128]{0,1:T(8,128)}) %all-reduce.23.cloned.1.call-update) | async-done | bytes 65552 | tf_op jit(solution)/shard_map/psum | solution.py:155
  438.4 11.7 %cholesky.17 = f32[128,128]{1,0:T(8,128)S(1)} custom-call(f32[128,128]{1,0:T(8,128)S(1)} %fusion.67), custom_call_target="Cholesky" | custom-call | tf_op jit(solution)/shard_map/jit(cholesky)/cholesky | solution.py:156
  451.4 9.8 %custom-call.7 = f32[1,128,128]{1,2,0:T(8,128)S(1)} custom-call(f32[1,128,128]{2,1,0:T(8,128)S(1)} %fusion.65), custom_call_target="InvertDiagBlocksLowerTriangular" | custom-call | tf_op jit(solution)/shard_map/jit(_solve_triangular)/triangular_solve | solution.py:157
  461.5 4.7 fusion.10
  468.1 4.5 collective-permute-start
  475.8 3.1 fusion.44
  479.0 9.9 %fusion.37 = f32[1,256,128]{1,2,0:T(8,128)S(1)} fusion(f32[256,3,2,1024]{3,2,1,0:T(2,128)} %param.5, f32[128,3,2,1024]{3,0,2,1:T(8,128)S(1)} %fusion.10, f32[2,1024]{1,0:T(2,128)S(1)} %select_reduce_fusion), kind=kOutput, calls=%fused_computation.32 | convolution fusion | flops 2416705536 | bytes 9576448 | tf_op jit(solution)/shard_map/dot_general | solution.py:26
  488.9 7.2 %fusion.32 = f32[1,256,128]{1,2,0:T(8,128)S(1)} fusion(f32[256,3,2,1024]{3,2,1,0:T(2,128)S(1)} %bitcast.109, f32[128,3,2,1024]{3,0,2,1:T(8,128)S(1)} %fusion.10, f32[3,2,1024]{2,1,0:T(2,128)S(1)} %copy-done.15), kind=kOutput, calls=%fused_computation.31 | convolution fusion | flops 2416705536 | bytes 9592832 | tf_op jit(solution)/shard_map/dot_general | solution.py:26
  496.2 41.0 %collective-permute-done = f32[128,3,1,1024]{3,0,2,1:T(8,128)} collective-permute-done((f32[128,3,1,1024]{3,0,2,1:T(8,128)}, f32[128,3,1,1024]{3,0,2,1:T(8,128)}, u32[]{:S(2)}, u32[]{:S(2)}) %collective-permute-start) | collective-permute-done | bytes 1572896 | tf_op jit(solution)/shard_map/ppermute | solution.py:17
  537.2 2.7 pad_maximum_fusion
  541.1 2.6 fusion.76
  543.7 2.4 fusion.77
  546.5 3.4 fusion.59
  553.0 7.3 %fusion.29 = f32[1,256,128]{1,2,0:T(8,128)S(1)} fusion(f32[256,3,2,1024]{3,2,1,0:T(2,128)S(1)} %bitcast.109, f32[128,1,2,1024]{3,0,2,1:T(8,128)S(1)} %add_bitcast_fusion, f32[128,1,2,1024]{3,0,2,1:T(8,128)S(1)} %fusion.54, f32[128,1,2,1024]{3,0,2,1:T(8,128)S(1)} %get-tuple-element.19), kind=kOutput, calls=%fused_computation.30 | convolution fusion | flops 2417491968 | bytes 9568256 | tf_op jit(solution)/shard_map/dot_general | solution.py:26
  561.2 4.4 fusion.47
  567.1 3.1 fusion.43
  570.3 37.2 %psum.39 = f32[3,32,128]{2,1,0:T(8,128)} all-reduce(f32[3,32,128]{2,1,0:T(8,128)S(1)} %maximum_multiply_fusion), channel_id=1, replica_groups=mesh['grid'=8,'cols'=4] {'grid'}, use_global_device_ids=true, to_apply=%region_9.10 | all-reduce | flops 12288 | bytes 98304 | tf_op jit(solution)/shard_map/psum | solution.py:176
  607.5 26.2 %all-reduce.25.cloned.1.call-done = f32[3,256,128]{1,2,0:T(8,128)} async-done(((f32[3,256,128]{1,2,0:T(8,128)}), f32[3,256,128]{1,2,0:T(8,128)}) %all-reduce.25.cloned.1.call-update) | async-done | bytes 393232 | tf_op jit(solution)/shard_map/psum | solution.py:176
  (84 shorter events, 27.3 us)
Async XLA Ops:
  7.2 34.2 %all-gather.4.cloned.1.call-start = ((), (), s32[]{:S(2)}) async-start(), calls=%async_computation.2 | async-start | bytes 3932160 | tf_op jit(solution)/shard_map/all_gather | solution.py:146
  9.5 112.6 %all-reduce.19.cloned.1.call-start = ((), (), s32[]{:S(2)}) async-start(), calls=%async_computation.3 | async-start | bytes 262144 | tf_op jit(solution)/shard_map/psum | solution.py:147
  52.2 118.5 %reduce-scatter.3.cloned.1.call-start = ((), (), s32[]{:S(2)}) async-start(), calls=%async_computation.4 | async-start | bytes 3932160 | tf_op jit(solution)/shard_map/reduce_scatter | solution.py:148
  133.3 37.4 %copy-start.12 = (f32[32,3,2,1024]{3,2,1,0:T(2,128)S(1)}, f32[32,3,2,1024]{3,2,1,0:T(2,128)}, u32[]{:S(2)}) copy-start(f32[32,3,2,1024]{3,2,1,0:T(2,128)} %param.6) | copy-start | bytes 2359300
  133.3 68.4 %all-gather.6.cloned.1.call-start = ((), (), s32[]{:S(2)}) async-start(), calls=%async_computation.5 | async-start | bytes 3932160 | tf_op jit(solution)/shard_map/all_gather | solution.py:146
  173.0 109.2 %all-reduce.21.cloned.1.call-start = ((), (), s32[]{:S(2)}) async-start(), calls=%async_computation.6 | async-start | bytes 262144 | tf_op jit(solution)/shard_map/psum | solution.py:147
  212.4 118.5 %reduce-scatter.5.cloned.1.call-start = ((), (), s32[]{:S(2)}) async-start(), calls=%async_computation.7 | async-start | bytes 3932160 | tf_op jit(solution)/shard_map/reduce_scatter | solution.py:148
  293.5 37.4 %copy-start.3 = (f32[32,3,2,1024]{3,0,2,1:T(8,128)S(1)}, f32[32,3,2,1024]{3,0,2,1:T(8,128)}, u32[]{:S(2)}) copy-start(f32[32,3,2,1024]{3,0,2,1:T(8,128)} %copy_subtract_fusion) | copy-start | bytes 2359300
  293.5 68.2 %all-gather.8.cloned.1.call-start = ((), (), s32[]{:S(2)}) async-start(), calls=%async_computation.8 | async-start | bytes 3932160 | tf_op jit(solution)/shard_map/all_gather | solution.py:152
  333.0 103.6 %all-reduce.23.cloned.1.call-start = ((), (), s32[]{:S(2)}) async-start(), calls=%async_computation.9 | async-start | bytes 131072 | tf_op jit(solution)/shard_map/psum | solution.py:155
  361.7 6.4 copy-start
  368.0 265.7 %all-reduce.25.cloned.1.call-start = ((), (), s32[]{:S(2)}) async-start(), calls=%async_computation.10 | async-start | bytes 786432 | tf_op jit(solution)/shard_map/psum | solution.py:176
  466.2 7.9 %copy-start.16 = (s32[2,1024]{1,0:T(2,128)S(1)}, s32[2,1024]{1,0:T(2,128)}, u32[]{:S(2)}) copy-start(s32[2,1024]{1,0:T(2,128)} %param.8) | copy-start | bytes 24580
  466.2 7.9 %copy-start.17 = (f32[8]{0:T(128)S(1)}, f32[8]{0:T(128)}, u32[]{:S(2)}) copy-start(f32[8]{0:T(128)} %param.9) | copy-start | bytes 100
  466.2 8.0 %copy-start.13 = (f32[256,128]{1,0:T(8,128)S(1)}, f32[256,128]{1,0:T(8,128)}, u32[]{:S(2)}) copy-start(f32[256,128]{1,0:T(8,128)} %all-reduce.19.cloned.1.call-done) | copy-start | bytes 393220
  466.2 8.0 %copy-start.14 = (f32[256,128]{1,0:T(8,128)S(1)}, f32[256,128]{1,0:T(8,128)}, u32[]{:S(2)}) copy-start(f32[256,128]{1,0:T(8,128)} %all-reduce.21.cloned.1.call-done) | copy-start | bytes 393220
  466.2 9.6 %copy-start.15 = (f32[3,2,1024]{2,1,0:T(2,128)S(1)}, f32[3,2,1024]{2,1,0:T(2,128)}, u32[]{:S(2)}) copy-start(f32[3,2,1024]{2,1,0:T(2,128)} %param.7) | copy-start | bytes 73732
  468.1 69.1 %collective-permute-start = (f32[128,3,1,1024]{3,0,2,1:T(8,128)}, f32[128,3,1,1024]{3,0,2,1:T(8,128)}, u32[]{:S(2)}, u32[]{:S(2)}) collective-permute-start(f32[128,3,1,1024]{3,0,2,1:T(8,128)} %get-tuple-element.21), channel_id=1, source_target_pairs={{0,4},{4,8},{8,12},{12,16},{16,20},{20,24},{24,28},{1,5},{5,9},{9,... | collective-permute-start | bytes 4718600 | tf_op jit(solution)/shard_map/ppermute | solution.py:17
  472.6 64.6 %collective-permute-start.1 = (f32[128,3,1,1024]{3,0,2,1:T(8,128)}, f32[128,3,1,1024]{3,0,2,1:T(8,128)}, u32[]{:S(2)}, u32[]{:S(2)}) collective-permute-start(f32[128,3,1,1024]{3,0,2,1:T(8,128)} %get-tuple-element.22), channel_id=1, source_target_pairs={{4,0},{8,4},{12,8},{16,12},{20,16},{24,20},{28,24},{5,1},{9,5},{13... | collective-permute-start | bytes 4718600 | tf_op jit(solution)/shard_map/ppermute | solution.py:18
  475.0 0.9 copy-start.1
  475.8 13.0 %slice-start = ((s8[6291456]{0:T(1024)(128)(4,1)}), s8[4194304]{0:T(1024)(128)(4,1)S(1)}, s32[]{:S(2)}) async-start(s8[6291456]{0:T(1024)(128)(4,1)} %bitcast.108), calls=%async_computation.11 | async-start | bytes 8388608
  479.0 9.9 %slice-start.1 = ((s8[6291456]{0:T(1024)(128)(4,1)}), s8[2097152]{0:T(1024)(128)(4,1)S(1)}, s32[]{:S(2)}) async-start(s8[6291456]{0:T(1024)(128)(4,1)} %bitcast.108), calls=%async_computation.12 | async-start | bytes 4194304
  549.8 3.2 copy-start.6
  549.8 1.6 copy-start.8
  549.8 1.9 copy-start.11
  551.2 1.8 copy-start.4
  553.0 7.3 %copy-start.9 = (f32[128,1,2,1024]{3,0,2,1:T(8,128)}, f32[128,1,2,1024]{3,0,2,1:T(8,128)S(1)}, u32[]{:S(2)}) copy-start(f32[128,1,2,1024]{3,0,2,1:T(8,128)S(1)} %add_bitcast_fusion) | copy-start | bytes 3145732
  561.1 4.5 copy-start.2
  561.1 6.0 copy-start.5
  561.1 6.0 copy-start.7
  561.1 6.0 copy-start.10
Sparse Core Ops, SparseCore 0:
  10.1 31.2 all-gather.3
  52.3 69.6 all-reduce.18
  133.4 37.2 reduce-scatter.2
  173.1 28.5 all-gather.5
  212.5 69.6 all-reduce.20
  293.6 37.2 reduce-scatter.4
  333.1 28.5 all-gather.7
  368.1 68.4 all-reduce.22
  561.2 72.4 all-reduce.24
where the time goes:
time: 652 us; the launch traced here: 643 us
  waiting for transfers between devices  421 us (65%)
  matrix products  90.2 us (14%)
  other arithmetic  38.7 us (6%)
  blocking collectives  37.2 us (6%)
  local copies, waits for them, and re-layouts  34 us (5%)
  between operations  14.7 us (2%)
  starting transfers between devices  6.98 us (1%)
    psum x2, waiting for transfers between devices, shards(): coef_part = lax.psum(partial_value, 'grid')  124 us
    reduce_scatter x2, waiting for transfers between devices, shards(): lax.psum_scatter(combine_rows(coef_part, basis), 'cols', scatter_dimensio...  74.4 us
    psum x1, waiting for transfers between devices, shards(): gram_sum = lax.psum(cells_dot(finished, finished) / unknowns, 'grid')  66.2 us
    dot_general x9, matrix products, cells_dot(): lax.dot_general(left_flat, right_flat, (((1,), (1,)), ((), ())), precisio...  62.8 us
    all_gather x2, waiting for transfers between devices, shards(): lax.all_gather(current, 'cols', axis=0, tiled=True)  60.5 us
    ppermute x1, waiting for transfers between devices, padded(): before = lax.ppermute(last, axis, up)  41 us
    psum x1, blocking collectives, shards(): cross_terms, block_terms = lax.psum((cross_part, block_part), 'grid')  37.2 us
    all_gather x1, waiting for transfers between devices, shards(): finished = lax.all_gather(current, 'cols', axis=0, tiled=True)  28.2 us
  transfers between devices with their start and end apart: 11, of which 10 were waited for; matrix products, arithmetic and copies ran while one was open for 7% of the time, Pallas kernels for 0%

commit v1 on v0

--- a/solution.py
+++ b/solution.py
@@ -144,7 +144,11 @@
     coefficients = jnp.zeros((basis_cols, total_snap), jnp.float32)
     for sweep_index in range(2):
         partial_value = cells_dot(basis, lax.all_gather(current, "cols", axis=0, tiled=True))
-        coef_part = lax.psum(partial_value, "grid")
+        coef_part = partial_value
+        for hop in (1, 2, 4):
+            coef_part = coef_part + lax.ppermute(
+                coef_part, "grid", [(dev, dev ^ hop) for dev in range(8)]
+            )
         current = current - lax.psum_scatter(
             combine_rows(coef_part, basis), "cols", scatter_dimension=0, tiled=True
         )

time: 652 us -> 558 us (0.86)
  waiting for transfers between devices: 421 us -> 315 us
  starting transfers between devices: 6.98 us -> 18 us
    psum x2 -> x0, waiting for transfers between devices: 124 us -> none  [shards(): coef_part = lax.psum(partial_value, 'grid')]
    ppermute x0 -> x6, waiting for transfers between devices: none -> 20.3 us  [shards(): lax.ppermute(coef_part, 'grid', [(dev, dev ^ hop) for dev in range(8)])]
    ppermute x0 -> x6, starting transfers between devices: none -> 11.1 us  [shards(): lax.ppermute(coef_part, 'grid', [(dev, dev ^ hop) for dev in range(8)])]
  transfers between devices with their start and end apart: 11 -> 15, of which waited for: 10 -> 13; matrix products, arithmetic and copies ran while one was open for 7% -> 9% of each run, Pallas kernels for 0% -> 0%
where the time goes in v1:
time: 558 us; the launch traced here: 548 us
  waiting for transfers between devices  315 us (56%)
  matrix products  89.6 us (16%)
  other arithmetic  39.5 us (7%)
  blocking collectives  37.2 us (7%)
  local copies, waits for them, and re-layouts  34 us (6%)
  starting transfers between devices  18 us (3%)
  between operations  15 us (3%)
    reduce_scatter x2, waiting for transfers between devices, shards(): lax.psum_scatter(combine_rows(coef_part, basis), 'cols', scatter_dimensio...  74.2 us
    psum x1, waiting for transfers between devices, shards(): gram_sum = lax.psum(cells_dot(finished, finished) / unknowns, 'grid')  65 us
    dot_general x9, matrix products, cells_dot(): lax.dot_general(left_flat, right_flat, (((1,), (1,)), ((), ())), precisio...  62.5 us
    all_gather x2, waiting for transfers between devices, shards(): lax.all_gather(current, 'cols', axis=0, tiled=True)  60.3 us
    ppermute x1, waiting for transfers between devices, padded(): before = lax.ppermute(last, axis, up)  40.3 us
    psum x1, blocking collectives, shards(): cross_terms, block_terms = lax.psum((cross_part, block_part), 'grid')  37.2 us
    all_gather x1, waiting for transfers between devices, shards(): finished = lax.all_gather(current, 'cols', axis=0, tiled=True)  28.6 us
    dot_general x3, matrix products, combine_rows(): lax.dot_general(weights, flattened, (((0,), (0,)), ((), ())), precision=H...  26.9 us
  transfers between devices with their start and end apart: 15, of which 13 were waited for; matrix products, arithmetic and copies ran while one was open for 9% of the time, Pallas kernels for 0%

profile of v1, /device:TPU:0, one launch (start us, length us, event | category | flops | bytes accessed | tf_op | source)
XLA Modules:
  0.0 548.3 jit_solution(4930944442206233257)
XLA Ops:
  9.5 31.9 %all-gather.4.cloned.1.call-done = f32[128,3,2,1024]{3,0,2,1:T(8,128)} async-done(((f32[32,3,2,1024]{3,0,2,1:T(8,128)}), f32[128,3,2,1024]{3,0,2,1:T(8,128)}) %all-gather.4.cloned.1.call-update) | async-done | bytes 3145744 | tf_op jit(solution)/shard_map/all_gather | solution.py:146
  41.4 10.2 %fusion.23 = f32[256,128]{1,0:T(8,128)S(1)} fusion(f32[128,3,2,1024]{3,0,2,1:T(8,128)} %all-gather.4.cloned.1.call-done, f32[256,3,2,1024]{3,2,1,0:T(2,128)} %param.5), kind=kOutput, calls=%fused_computation.28 | convolution fusion | flops 2415919104 | bytes 9568256 | tf_op jit(solution)/shard_map/dot_general | solution.py:26
  53.1 4.2 collective-permute-done
  58.8 3.5 collective-permute-done.1
  64.8 9.0 %reshape.49 = f32[256,6144]{1,0:T(8,128)} reshape(f32[256,3,2,1024]{3,2,1,0:T(2,128)} %param.5) | data formatting | bytes 12582912 | tf_op jit(solution)/shard_map/reshape | solution.py:24
  73.8 6.6 %copy.42 = f32[6144,256]{1,0:T(8,128)} copy(f32[6144,256]{0,1:T(8,128)} %bitcast.112) | data formatting | bytes 12582912 | tf_op jit(solution)/shard_map/dot_general | solution.py:37
  80.4 11.1 %fusion.63 = f32[128,3,2,1024]{3,0,2,1:T(8,128)} fusion(f32[3,2,1024,256]{3,2,1,0:T(8,128)} %bitcast.110, f32[256,128]{1,0:T(8,128)S(1)} %add.146), kind=kOutput, calls=%fused_computation.61 | convolution fusion | flops 2415919104 | bytes 9568256 | tf_op jit(solution)/shard_map/dot_general | solution.py:37
  91.6 36.2 %reduce-scatter.3.cloned.1.call-done = f32[32,3,2,1024]{3,0,2,1:T(8,128)} async-done(((f32[128,3,2,1024]{3,0,2,1:T(8,128)}), f32[32,3,2,1024]{3,0,2,1:T(8,128)}) %reduce-scatter.3.cloned.1.call-update) | async-done | bytes 786448 | tf_op jit(solution)/shard_map/reduce_scatter | solution.py:152
  130.4 28.4 %all-gather.6.cloned.1.call-done = f32[128,3,2,1024]{3,0,2,1:T(8,128)} async-done(((f32[32,3,2,1024]{3,0,2,1:T(8,128)}), f32[128,3,2,1024]{3,0,2,1:T(8,128)}) %all-gather.6.cloned.1.call-update) | async-done | bytes 3145744 | tf_op jit(solution)/shard_map/all_gather | solution.py:146
  158.8 10.1 %fusion.26 = f32[256,128]{1,0:T(8,128)S(1)} fusion(f32[128,3,2,1024]{3,0,2,1:T(8,128)} %all-gather.6.cloned.1.call-done, f32[256,3,2,1024]{3,2,1,0:T(2,128)} %param.5), kind=kOutput, calls=%fused_computation.29 | convolution fusion | flops 2415919104 | bytes 9568256 | tf_op jit(solution)/shard_map/dot_general | solution.py:26
  170.4 4.2 collective-permute-done.3
  176.2 3.5 collective-permute-done.4
  182.1 5.0 collective-permute-done.5
  187.1 11.1 %fusion.61 = f32[128,3,2,1024]{3,0,2,1:T(8,128)} fusion(f32[3,2,1024,256]{3,2,1,0:T(8,128)} %bitcast.111, f32[256,128]{1,0:T(8,128)S(1)} %add.148, f32[256,128]{1,0:T(8,128)S(1)} %collective-permute-done.5), kind=kOutput, calls=%fused_computation.59 | convolution fusion | flops 2415951872 | bytes 9699328 | tf_op jit(solution)/shard_map/dot_general | solution.py:37
  198.3 38.0 %reduce-scatter.5.cloned.1.call-done = f32[32,3,2,1024]{3,0,2,1:T(8,128)} async-done(((f32[128,3,2,1024]{3,0,2,1:T(8,128)}), f32[32,3,2,1024]{3,0,2,1:T(8,128)}) %reduce-scatter.5.cloned.1.call-update) | async-done | bytes 786448 | tf_op jit(solution)/shard_map/reduce_scatter | solution.py:152
  238.5 28.6 %all-gather.8.cloned.1.call-done = f32[128,3,2,1024]{3,0,2,1:T(8,128)} async-done(((f32[32,3,2,1024]{3,0,2,1:T(8,128)}), f32[128,3,2,1024]{3,0,2,1:T(8,128)}) %all-gather.8.cloned.1.call-update) | async-done | bytes 3145744 | tf_op jit(solution)/shard_map/all_gather | solution.py:156
  267.1 6.3 %fusion.42 = f32[128,128]{0,1:T(8,128)} fusion(f32[128,3,2,1024]{3,0,2,1:T(8,128)} %all-gather.8.cloned.1.call-done), kind=kOutput, calls=%fused_computation.35 | convolution fusion | flops 1207975936 | bytes 3211264 | tf_op jit(solution)/shard_map/dot_general | solution.py:26
  277.0 65.0 %all-reduce.17.cloned.1.call-done = f32[128,128]{0,1:T(8,128)} async-done(((f32[128,128]{0,1:T(8,128)}), f32[128,128]{0,1:T(8,128)}) %all-reduce.17.cloned.1.call-update) | async-done | bytes 65552 | tf_op jit(solution)/shard_map/psum | solution.py:159
  343.8 11.7 %cholesky.17 = f32[128,128]{1,0:T(8,128)S(1)} custom-call(f32[128,128]{1,0:T(8,128)S(1)} %fusion.67), custom_call_target="Cholesky" | custom-call | tf_op jit(solution)/shard_map/jit(cholesky)/cholesky | solution.py:160
  356.9 9.8 %custom-call.7 = f32[1,128,128]{1,2,0:T(8,128)S(1)} custom-call(f32[1,128,128]{2,1,0:T(8,128)S(1)} %fusion.65), custom_call_target="InvertDiagBlocksLowerTriangular" | custom-call | tf_op jit(solution)/shard_map/jit(_solve_triangular)/triangular_solve | solution.py:161
  367.0 4.7 fusion.10
  373.5 4.5 collective-permute-start.6
  381.1 4.0 fusion.44
  385.2 9.9 %fusion.37 = f32[1,256,128]{1,2,0:T(8,128)S(1)} fusion(f32[256,3,2,1024]{3,2,1,0:T(2,128)} %param.5, f32[128,3,2,1024]{3,0,2,1:T(8,128)S(1)} %fusion.10, f32[2,1024]{1,0:T(2,128)S(1)} %select_reduce_fusion), kind=kOutput, calls=%fused_computation.32 | convolution fusion | flops 2416705536 | bytes 9576448 | tf_op jit(solution)/shard_map/dot_general | solution.py:26
  395.1 7.2 %fusion.32 = f32[1,256,128]{1,2,0:T(8,128)S(1)} fusion(f32[256,3,2,1024]{3,2,1,0:T(2,128)S(1)} %bitcast.109, f32[128,3,2,1024]{3,0,2,1:T(8,128)S(1)} %fusion.10, f32[3,2,1024]{2,1,0:T(2,128)S(1)} %copy-done.13), kind=kOutput, calls=%fused_computation.31 | convolution fusion | flops 2416705536 | bytes 9592832 | tf_op jit(solution)/shard_map/dot_general | solution.py:26
  402.4 40.3 %collective-permute-done.6 = f32[128,3,1,1024]{3,0,2,1:T(8,128)} collective-permute-done((f32[128,3,1,1024]{3,0,2,1:T(8,128)}, f32[128,3,1,1024]{3,0,2,1:T(8,128)}, u32[]{:S(2)}, u32[]{:S(2)}) %collective-permute-start.6) | collective-permute-done | bytes 1572896 | tf_op jit(solution)/shard_map/ppermute | solution.py:17
  451.9 3.4 fusion.59
  458.4 7.3 %fusion.29 = f32[1,256,128]{1,2,0:T(8,128)S(1)} fusion(f32[256,3,2,1024]{3,2,1,0:T(2,128)S(1)} %bitcast.109, f32[128,1,2,1024]{3,0,2,1:T(8,128)S(1)} %add_bitcast_fusion, f32[128,1,2,1024]{3,0,2,1:T(8,128)S(1)} %fusion.54, f32[128,1,2,1024]{3,0,2,1:T(8,128)S(1)} %get-tuple-element.19), kind=kOutput, calls=%fused_computation.30 | convolution fusion | flops 2417491968 | bytes 9568256 | tf_op jit(solution)/shard_map/dot_general | solution.py:26
  466.5 4.4 fusion.47
  472.5 3.1 fusion.43
  475.6 37.2 %psum.23 = f32[3,32,128]{2,1,0:T(8,128)} all-reduce(f32[3,32,128]{2,1,0:T(8,128)S(1)} %maximum_multiply_fusion), channel_id=1, replica_groups=mesh['grid'=8,'cols'=4] {'grid'}, use_global_device_ids=true, to_apply=%region_7.8 | all-reduce | flops 12288 | bytes 98304 | tf_op jit(solution)/shard_map/psum | solution.py:180
  512.9 26.2 %all-reduce.19.cloned.1.call-done = f32[3,256,128]{1,2,0:T(8,128)} async-done(((f32[3,256,128]{1,2,0:T(8,128)}), f32[3,256,128]{1,2,0:T(8,128)}) %all-reduce.19.cloned.1.call-update) | async-done | bytes 393232 | tf_op jit(solution)/shard_map/psum | solution.py:180
  (89 shorter events, 46.8 us)
Async XLA Ops:
  7.2 34.2 %all-gather.4.cloned.1.call-start = ((), (), s32[]{:S(2)}) async-start(), calls=%async_computation.2 | async-start | bytes 3932160 | tf_op jit(solution)/shard_map/all_gather | solution.py:146
  9.5 118.3 %reduce-scatter.3.cloned.1.call-start = ((), (), s32[]{:S(2)}) async-start(), calls=%async_computation.3 | async-start | bytes 3932160 | tf_op jit(solution)/shard_map/reduce_scatter | solution.py:152
  51.6 5.7 %collective-permute-start = (f32[256,128]{1,0:T(8,128)S(1)}, f32[256,128]{1,0:T(8,128)S(1)}, u32[]{:S(2)}, u32[]{:S(2)}) collective-permute-start(f32[256,128]{1,0:T(8,128)S(1)} %fusion.23), channel_id=1, source_target_pairs={{0,4},{4,0},{8,12},{12,8},{16,20},{20,16},{24,28},{28,24},{1,5},{5... | collective-permute-start | bytes 393224 | tf_op jit(solution)/shard_map/ppermute | solution.py:149
  57.3 5.0 collective-permute-start.1
  62.3 18.0 %collective-permute-start.2 = (f32[256,128]{1,0:T(8,128)S(1)}, f32[256,128]{1,0:T(8,128)S(1)}, u32[]{:S(2)}, u32[]{:S(2)}) collective-permute-start(f32[256,128]{1,0:T(8,128)S(1)} %add.145), channel_id=1, source_target_pairs={{0,16},{4,20},{8,24},{12,28},{16,0},{20,4},{24,8},{28,12},{1,17},{... | collective-permute-start | bytes 393224 | tf_op jit(solution)/shard_map/ppermute | solution.py:149
  91.5 36.3 %copy-start.12 = (f32[32,3,2,1024]{3,2,1,0:T(2,128)S(1)}, f32[32,3,2,1024]{3,2,1,0:T(2,128)}, u32[]{:S(2)}) copy-start(f32[32,3,2,1024]{3,2,1,0:T(2,128)} %param.6) | copy-start | bytes 2359300
  91.6 67.3 %all-gather.6.cloned.1.call-start = ((), (), s32[]{:S(2)}) async-start(), calls=%async_computation.4 | async-start | bytes 3932160 | tf_op jit(solution)/shard_map/all_gather | solution.py:146
  130.2 106.2 %reduce-scatter.5.cloned.1.call-start = ((), (), s32[]{:S(2)}) async-start(), calls=%async_computation.5 | async-start | bytes 3932160 | tf_op jit(solution)/shard_map/reduce_scatter | solution.py:152
  168.9 5.7 %collective-permute-start.3 = (f32[256,128]{1,0:T(8,128)S(1)}, f32[256,128]{1,0:T(8,128)S(1)}, u32[]{:S(2)}, u32[]{:S(2)}) collective-permute-start(f32[256,128]{1,0:T(8,128)S(1)} %fusion.26), channel_id=1, source_target_pairs={{0,4},{4,0},{8,12},{12,8},{16,20},{20,16},{24,28},{28,24},{1,5},{5... | collective-permute-start | bytes 393224 | tf_op jit(solution)/shard_map/ppermute | solution.py:149
  174.6 5.0 collective-permute-start.4
  179.7 7.5 %collective-permute-start.5 = (f32[256,128]{1,0:T(8,128)S(1)}, f32[256,128]{1,0:T(8,128)S(1)}, u32[]{:S(2)}, u32[]{:S(2)}) collective-permute-start(f32[256,128]{1,0:T(8,128)S(1)} %add.148), channel_id=1, source_target_pairs={{0,16},{4,20},{8,24},{12,28},{16,0},{20,4},{24,8},{28,12},{1,17},{... | collective-permute-start | bytes 393224 | tf_op jit(solution)/shard_map/ppermute | solution.py:149
  198.2 38.1 %copy-start.3 = (f32[32,3,2,1024]{3,0,2,1:T(8,128)S(1)}, f32[32,3,2,1024]{3,0,2,1:T(8,128)}, u32[]{:S(2)}) copy-start(f32[32,3,2,1024]{3,0,2,1:T(8,128)} %copy_subtract_fusion) | copy-start | bytes 2359300
  198.3 68.9 %all-gather.8.cloned.1.call-start = ((), (), s32[]{:S(2)}) async-start(), calls=%async_computation.6 | async-start | bytes 3932160 | tf_op jit(solution)/shard_map/all_gather | solution.py:156
  238.4 35.5 %copy-start.14 = (s32[2,1024]{1,0:T(2,128)S(1)}, s32[2,1024]{1,0:T(2,128)}, u32[]{:S(2)}) copy-start(s32[2,1024]{1,0:T(2,128)} %param.8) | copy-start | bytes 24580
  238.5 103.6 %all-reduce.17.cloned.1.call-start = ((), (), s32[]{:S(2)}) async-start(), calls=%async_computation.7 | async-start | bytes 131072 | tf_op jit(solution)/shard_map/psum | solution.py:159
  267.1 7.5 %copy-start = (f32[128,3,2,1024]{3,0,2,1:T(8,128)S(1)}, f32[128,3,2,1024]{3,0,2,1:T(8,128)}, u32[]{:S(2)}) copy-start(f32[128,3,2,1024]{3,0,2,1:T(8,128)} %all-gather.8.cloned.1.call-done) | copy-start | bytes 9437188
  273.4 265.7 %all-reduce.19.cloned.1.call-start = ((), (), s32[]{:S(2)}) async-start(), calls=%async_computation.8 | async-start | bytes 786432 | tf_op jit(solution)/shard_map/psum | solution.py:180
  373.5 69.1 %collective-permute-start.6 = (f32[128,3,1,1024]{3,0,2,1:T(8,128)}, f32[128,3,1,1024]{3,0,2,1:T(8,128)}, u32[]{:S(2)}, u32[]{:S(2)}) collective-permute-start(f32[128,3,1,1024]{3,0,2,1:T(8,128)} %get-tuple-element.21), channel_id=1, source_target_pairs={{0,4},{4,8},{8,12},{12,16},{16,20},{20,24},{24,28},{1,5},{5,9},{9,... | collective-permute-start | bytes 4718600 | tf_op jit(solution)/shard_map/ppermute | solution.py:17
  378.0 64.6 %collective-permute-start.7 = (f32[128,3,1,1024]{3,0,2,1:T(8,128)}, f32[128,3,1,1024]{3,0,2,1:T(8,128)}, u32[]{:S(2)}, u32[]{:S(2)}) collective-permute-start(f32[128,3,1,1024]{3,0,2,1:T(8,128)} %get-tuple-element.22), channel_id=1, source_target_pairs={{4,0},{8,4},{12,8},{16,12},{20,16},{24,20},{28,24},{5,1},{9,5},{13... | collective-permute-start | bytes 4718600 | tf_op jit(solution)/shard_map/ppermute | solution.py:18
  380.2 0.9 copy-start.1
  381.1 13.9 %slice-start = ((s8[6291456]{0:T(1024)(128)(4,1)}), s8[4194304]{0:T(1024)(128)(4,1)S(1)}, s32[]{:S(2)}) async-start(s8[6291456]{0:T(1024)(128)(4,1)} %bitcast.108), calls=%async_computation.9 | async-start | bytes 8388608
  385.2 9.9 %slice-start.1 = ((s8[6291456]{0:T(1024)(128)(4,1)}), s8[2097152]{0:T(1024)(128)(4,1)S(1)}, s32[]{:S(2)}) async-start(s8[6291456]{0:T(1024)(128)(4,1)} %bitcast.108), calls=%async_computation.10 | async-start | bytes 4194304
  385.2 9.9 %copy-start.13 = (f32[3,2,1024]{2,1,0:T(2,128)S(1)}, f32[3,2,1024]{2,1,0:T(2,128)}, u32[]{:S(2)}) copy-start(f32[3,2,1024]{2,1,0:T(2,128)} %param.7) | copy-start | bytes 73732
  455.2 3.2 copy-start.6
  455.2 1.6 copy-start.8
  455.2 1.9 copy-start.11
  456.6 1.8 copy-start.4
  458.4 7.3 %copy-start.9 = (f32[128,1,2,1024]{3,0,2,1:T(8,128)}, f32[128,1,2,1024]{3,0,2,1:T(8,128)S(1)}, u32[]{:S(2)}) copy-start(f32[128,1,2,1024]{3,0,2,1:T(8,128)S(1)} %add_bitcast_fusion) | copy-start | bytes 3145732
  466.5 4.5 copy-start.2
  466.5 6.0 %copy-start.5 = (f32[128,1,2,1024]{3,0,2,1:T(8,128)S(1)}, f32[128,1,2,1024]{3,0,2,1:T(8,128)}, u32[]{:S(2)}) copy-start(f32[128,1,2,1024]{3,0,2,1:T(8,128)} %copy-done.4) | copy-start | bytes 3145732
  466.5 6.0 %copy-start.7 = (f32[128,1,2,1024]{3,0,2,1:T(8,128)S(1)}, f32[128,1,2,1024]{3,0,2,1:T(8,128)}, u32[]{:S(2)}) copy-start(f32[128,1,2,1024]{3,0,2,1:T(8,128)} %copy-done.6) | copy-start | bytes 3145732
  466.5 6.0 %copy-start.10 = (f32[128,1,2,1024]{3,0,2,1:T(8,128)S(1)}, f32[128,1,2,1024]{3,0,2,1:T(8,128)}, u32[]{:S(2)}) copy-start(f32[128,1,2,1024]{3,0,2,1:T(8,128)} %copy-done.9) | copy-start | bytes 3145732
Sparse Core Ops, SparseCore 0:
  10.1 31.2 all-gather.3
  91.7 36.0 reduce-scatter.2
  130.3 28.5 all-gather.5
  198.4 37.8 reduce-scatter.4
  238.6 28.5 all-gather.7
  273.6 68.4 all-reduce.16
  466.6 72.4 all-reduce.18
